TPU v7x, 32 devices: a whole 2x2x4 slice. The times are simulated.
32 devices in a mesh: parts: 2 (over x), blk: 16 (over z, y, core).
Axes of the slice: x: 2, y: 2, z: 4, core: 2. Of those that a mesh axis runs over, the one named last changes fastest.
Arguments:
- queries: bfloat16 [512, 8192], P('blk'), may hold values from -6 to 6
- train_grads: bfloat16 [16384, 8192], P(('parts', 'blk')), parts along dimension 0, may hold values from -0.0625 to 0.0625
- group_of: int32 [8], replicated, may hold values from 0 to 7, each once
- basis_out: float32 [8, 32, 32], replicated, may hold values from -1 to 1
- basis_in: float32 [8, 32, 32], replicated, may hold values from -1 to 1
- eigen: float32 [8, 32, 32], replicated, may hold values from 0.1 to 10
- store_ids: int32 [16384], P('parts'), parts along dimension 0, may hold values from 0 to 8191, each once
Outputs:
- influence: bfloat16 [512, 16384], P('blk', 'parts'), parts along dimension 1
There are 2 independent parts, one for each index of `parts`. A program takes and returns all parts, laid end to end along the dimension named above; an argument that names none is the same for every part. Nothing has to cross between parts.
Inputs may be any that keep to these rules, and one draw needn't show every extreme that they name: `group_of`: each layer group serves exactly one block. `store_ids`: every example id appears once.
All inputs are finite; a program needn't handle non-finite values.
Results may differ from a plain program's by a relative error of at most 0.0049.
Values may be sent and summed in bfloat16 or wider, within the bound.
A program may use at most 128 MiB of HBM per device.

v0:
```python
import functools

import jax
import jax.numpy as jnp
from jax import lax
from jax.experimental import pallas as pl
from jax.experimental.pallas import tpu as pltpu
from jax.sharding import PartitionSpec as P

damping_share = 0.1
LANES = 128
WIDE = 256


def pieces(values, count):
    parts = []
    for _ in range(count):
        part = values.astype(jnp.bfloat16)
        parts.append(part)
        values = values - part.astype(jnp.float32)
    return parts


def mxu(left, right):
    return lax.dot_general(
        left, right, (((1,), (0,)), ((), ())), preferred_element_type=jnp.float32
    )


def condition_kernel(order, group_ref, x_ref, bases_ref, eigen_ref, out_ref):
    del group_ref
    rows = x_ref.shape[0]
    per = LANES // order
    chunks = order // per
    bases = bases_ref[0]
    lane = lax.broadcasted_iota(jnp.int32, (order, order * order), 1)
    line = lax.broadcasted_iota(jnp.int32, (order, order * order), 0)
    spread = jnp.where(lane // order == line, 1.0, 0.0).astype(jnp.bfloat16)
    lane = lax.broadcasted_iota(jnp.int32, (order, LANES), 1)
    line = lax.broadcasted_iota(jnp.int32, (order, LANES), 0)
    repeat = jnp.where(lane % order == line, 1.0, 0.0).astype(jnp.bfloat16)

    first = 2 * order
    wide = mxu(jnp.concatenate(pieces(bases[:first], 3), axis=0), spread)
    wide = wide[:first] + wide[first : 2 * first] + wide[2 * first :]
    wide_out, wide_back = wide[:order], wide[order:]
    tall = mxu(jnp.concatenate(pieces(bases[first:], 2), axis=0), repeat)
    forward_high, back_high = tall[:order], tall[order : 2 * order]
    forward_low, back_low = tall[2 * order : 3 * order], tall[3 * order :]

    def placed(tile):
        blank = jnp.zeros_like(tile)
        return jnp.concatenate(
            [
                jnp.concatenate([tile if k == p else blank for k in range(per)], axis=0)
                for p in range(per)
            ],
            axis=1,
        ).astype(jnp.bfloat16)

    def mix(spread_rows, coefficients):
        totals = [jnp.zeros((rows, LANES), jnp.float32) for _ in range(chunks)]
        for c in range(chunks):
            for p in range(per):
                s = c * per + p
                value = spread_rows[c * rows : (c + 1) * rows, p * LANES : (p + 1) * LANES]
                for k in range(chunks):
                    weight = coefficients[s : s + 1, k * LANES : (k + 1) * LANES]
                    totals[k] = totals[k] + weight * value
        return totals

    x = x_ref[...].astype(jnp.float32)
    x = jnp.concatenate(
        [x[:, c * LANES : (c + 1) * LANES] for c in range(chunks)], axis=0
    ).astype(jnp.bfloat16)
    right = jnp.concatenate([placed(forward_high), placed(forward_low)], axis=0)
    rotated = mix(mxu(jnp.concatenate([x, x], axis=1), right), wide_out)

    eigen = eigen_ref[0]
    total = jnp.sum(jnp.sum(eigen, axis=1, keepdims=True), axis=0, keepdims=True)
    spectrum = eigen + damping_share * (total * (1.0 / (order * order)))
    scaled = jnp.concatenate(
        [rotated[k] / spectrum[k : k + 1] for k in range(chunks)], axis=0
    )
    high, low = pieces(scaled, 2)
    back = placed(back_high)
    restored = mxu(
        jnp.concatenate([high, low], axis=1), jnp.concatenate([back, back], axis=0)
    ) + mxu(high, placed(back_low))
    for k, total in enumerate(mix(restored, wide_back)):
        out_ref[:, k * LANES : (k + 1) * LANES] = total.astype(jnp.bfloat16)


def condition(queries, group_of, basis_out, basis_in, eigen):
    groups, order, _ = eigen.shape
    rows = queries.shape[0]
    size = order * order
    bases = jnp.concatenate(
        [basis_out, jnp.swapaxes(basis_out, 1, 2), basis_in, jnp.swapaxes(basis_in, 1, 2)],
        axis=1,
    )
    return pl.pallas_call(
        functools.partial(condition_kernel, order),
        grid_spec=pltpu.PrefetchScalarGridSpec(
            num_scalar_prefetch=1,
            grid=(groups,),
            in_specs=[
                pl.BlockSpec((rows, size), lambda b, g: (0, b)),
                pl.BlockSpec((1, 4 * order, order), lambda b, g: (g[b], 0, 0)),
                pl.BlockSpec((1, size // LANES, LANES), lambda b, g: (g[b], 0, 0)),
            ],
            out_specs=pl.BlockSpec((rows, size), lambda b, g: (0, b)),
        ),
        out_shape=jax.ShapeDtypeStruct(queries.shape, jnp.bfloat16),
        compiler_params=pltpu.CompilerParams(vmem_limit_bytes=32 * 1024 * 1024),
        name="condition",
    )(group_of, queries, bases, eigen.reshape(groups, size // LANES, LANES))


def arrange_kernel(scores_ref, ids_ref, out_ref, total):
    step = pl.program_id(0)
    rows, count = scores_ref.shape[1:]
    groups = out_ref.shape[1] // WIDE
    ids = ids_ref[0]
    coarse = ids // WIDE
    fine = ids % WIDE
    scores = scores_ref[0].astype(jnp.float32)
    left = jnp.concatenate(
        [jnp.where(coarse == h, scores, 0.0) for h in range(groups)], axis=0
    ).astype(jnp.bfloat16)
    line = lax.broadcasted_iota(jnp.int32, (WIDE, count), 0)
    chosen = jnp.where(line == fine, 1.0, 0.0).astype(jnp.bfloat16)
    term = lax.dot_general(
        left, chosen, (((1,), (1,)), ((), ())), preferred_element_type=jnp.float32
    )

    @pl.when(step == 0)
    def _():
        total[...] = term

    @pl.when(step > 0)
    def _():
        total[...] += term

    @pl.when(step == pl.num_programs(0) - 1)
    def _():
        for h in range(groups):
            out_ref[:, h * WIDE : (h + 1) * WIDE] = total[
                h * rows : (h + 1) * rows, :
            ].astype(jnp.bfloat16)


def arrange(parted, ids):
    blocks, rows, count = parted.shape
    width = blocks * count
    return pl.pallas_call(
        arrange_kernel,
        grid=(blocks,),
        in_specs=[
            pl.BlockSpec((1, rows, count), lambda k: (k, 0, 0)),
            pl.BlockSpec((1, 1, count), lambda k: (k, 0, 0)),
        ],
        out_specs=pl.BlockSpec((rows, width), lambda k: (0, 0)),
        out_shape=jax.ShapeDtypeStruct((rows, width), jnp.bfloat16),
        scratch_shapes=[pltpu.VMEM((rows * (width // WIDE), WIDE), jnp.float32)],
        compiler_params=pltpu.CompilerParams(vmem_limit_bytes=32 * 1024 * 1024),
        name="arrange",
    )(parted, ids.reshape(blocks, 1, count))


def local(queries, train_grads, group_of, basis_out, basis_in, eigen, store_ids):
    conditioned = condition(queries, group_of, basis_out, basis_in, eigen)
    scores = lax.dot_general(
        lax.all_gather(conditioned, "blk", axis=0, tiled=True),
        train_grads,
        (((1,), (1,)), ((), ())),
        preferred_element_type=jnp.float32,
    ).astype(jnp.bfloat16)
    blocks = scores.shape[0] // queries.shape[0]
    parted = lax.all_to_all(
        scores.reshape(blocks, queries.shape[0], scores.shape[1]),
        "blk",
        split_axis=0,
        concat_axis=0,
    )
    return arrange(parted, store_ids)


def solution(mesh):
    return jax.shard_map(
        local,
        mesh=mesh,
        in_specs=(P("blk", None), P(("parts", "blk"), None), P(), P(), P(), P(), P("parts")),
        out_specs=P("blk", "parts"),
        check_vma=False,
    )
```

profile of v0, /device:TPU:0, one launch (start us, length us, event | category | flops | bytes accessed | tf_op | source)
XLA Modules:
  0.0 145.7 jit_solution(13994278080588544579)
XLA Ops:
  6.5 0.0 all-gather.2.cloned.1.call-start
  6.5 1.0 reshape.9.eigen_ref
  7.5 1.0 copy.13
  8.5 1.0 copy.14
  9.5 1.0 pad_maximum_fusion.bases_ref
  10.6 0.0 copy-start
  10.6 1.0 copy-done
  11.6 0.0 copy-start.2
  11.6 0.7 copy-done.2
  12.3 10.6 %condition.1 = bf16[32,8192]{1,0:T(8,128)(2,1)} custom-call(s32[8]{0:T(128)S(1)} %copy-done.2, bf16[32,8192]{1,0:T(8,128)(2,1)S(1)} %copy-done, f32[8,128,32]{2,1,0:T(8,128)S(1)} %pad_maximum_fusion.bases_ref, f32[8,8,128]{2,1,0:T(8,128)S(1)} %reshape.9.eigen_ref), custom_call_target="tpu_custom_call" | custom-call | tf_op jit(solution)/shard_map/condition/pallas_call | solution.py:102
  22.9 0.0 all-gather.2.cloned.1.call-update
  22.9 0.0 copy-start.1
  22.9 77.7 %all-gather.2.cloned.1.call-done = bf16[512,8192]{1,0:T(8,128)(2,1)} async-done(((bf16[32,8192]{1,0:T(8,128)(2,1)}), bf16[512,8192]{1,0:T(8,128)(2,1)}) %all-gather.2.cloned.1.call-update) | async-done | bytes 8388624 | tf_op jit(solution)/shard_map/all_gather | solution.py:174
  100.7 10.3 %convolution_convert_fusion = bf16[512,512]{1,0:T(8,128)(2,1)S(1)} fusion(bf16[512,8192]{1,0:T(8,128)(2,1)} %all-gather.2.cloned.1.call-done, bf16[512,8192]{1,0:T(8,128)(2,1)} %param.8), kind=kOutput, calls=%fused_computation | convolution fusion | flops 4295229440 | bytes 17301504 | tf_op jit(solution)/shard_map/dot_general | solution.py:173
  110.9 17.3 %all_to_all.5.scores_ref = bf16[16,32,512]{2,1,0:T(8,128)(2,1)S(1)} all-to-all(bf16[16,32,512]{2,1,0:T(8,128)(2,1)S(1)} %bitcast.7), channel_id=1, replica_groups=mesh['parts'=2,'blk'=16] {'blk'}, dimensions={0} | all-to-all | bytes 1048576 | tf_op jit(solution)/shard_map/all_to_all | solution.py:180
  128.2 0.0 copy-done.1
  128.2 10.6 %arrange.1 = bf16[32,8192]{1,0:T(8,128)(2,1)} custom-call(bf16[16,32,512]{2,1,0:T(8,128)(2,1)S(1)} %all_to_all.5.scores_ref, s32[16,1,512]{2,1,0:T(1,128)S(1)} %bitcast.6), custom_call_target="tpu_custom_call" | custom-call | tf_op jit(solution)/shard_map/arrange/pallas_call | solution.py:156
Async XLA Ops:
  6.5 94.1 %all-gather.2.cloned.1.call-start = ((), (), s32[]{:S(2)}) async-start(), calls=%async_computation.1 | async-start | bytes 8912896 | tf_op jit(solution)/shard_map/all_gather | solution.py:174
  10.6 1.0 copy-start
  11.6 0.7 copy-start.2
  22.9 105.3 %copy-start.1 = (s32[8192]{0:T(1024)S(1)}, s32[8192]{0:T(1024)}, u32[]{:S(2)}) copy-start(s32[8192]{0:T(1024)} %param.13) | copy-start | bytes 98308
Sparse Core Ops, SparseCore 0:
  23.0 77.5 all-gather.1
where the time goes:
time: 146 us
  waiting for transfers between devices  77.8 us (53%)
  Pallas kernels  21.2 us (15%)
  blocking collectives  17.3 us (12%)
  between operations  13.4 us (9%)
  matrix products  10.3 us (7%)
  local copies, waits for them, and re-layouts  4.69 us (3%)
    all_gather x1, waiting for transfers between devices, local(): lax.all_gather(conditioned, 'blk', axis=0, tiled=True)  77.7 us
    all_to_all x1, blocking collectives, local(): lax.all_to_all(scores.reshape(blocks, queries.shape[0], scores.shape[1]),...  17.3 us
    pallas_call x1, Pallas kernels, condition(): pl.pallas_call(functools.partial(condition_kernel, order), grid_spec=pltp...  10.6 us
    pallas_call x1, Pallas kernels, arrange(): pl.pallas_call(arrange_kernel, grid=(blocks,), in_specs=[pl.BlockSpec((1,...  10.6 us
    dot_general x1, matrix products, local(): lax.dot_general(lax.all_gather(conditioned, 'blk', axis=0, tiled=True), t...  10.3 us
    unnamed x8, local copies, waits for them, and re-layouts  3.7 us
  transfers between devices with their start and end apart: 1, of which 1 were waited for; matrix products, arithmetic and copies ran while one was open for 0% of the time, Pallas kernels for 0%

commit v1 on v0

--- a/solution.py
+++ b/solution.py
@@ -168,27 +168,229 @@
     )(parted, ids.reshape(blocks, 1, count))
 
 
-def local(queries, train_grads, group_of, basis_out, basis_in, eigen, store_ids):
-    conditioned = condition(queries, group_of, basis_out, basis_in, eigen)
+def ring_kernel(cores, x_ref, train_hbm, out_ref, held, train, total, stage, train_sem,
+                ring_send, ring_recv, twin_send, twin_recv, back_send, back_recv):
+    blocks, rows, count = out_ref.shape
+    half = rows // 2
+    depth = x_ref.shape[1]
+    chips = blocks // cores
+    long = chips // 2
+    subs = 2
+    part = depth // subs
+    quanta = 4
+    slice_of = depth // quanta
+    step_rows = 4 * half
+    pair = 2 * step_rows
+    me = lax.axis_index("blk")
+    core = me % cores
+    chip = me // cores
+    deep, side = chip // 2, chip % 2
+    place = deep + side * (2 * long - 1 - 2 * deep)
+
+    def device(position, its_core):
+        at_side = position // long
+        at_deep = position + at_side * (2 * long - 1 - 2 * position)
+        return (at_deep * 2 + at_side) * cores + its_core
+
+    onward = [device((place + 1) % chips, core), device((place + chips - 1) % chips, core)]
+    twin = device(place, 1 - core)
+
+    def rows_of(t, d, k):
+        return pl.ds(pl.multiple_of((t * 4 + d * 2 + k) * half, half), half)
+
+    def ring_copy(t, d, u):
+        columns = pl.ds(u * part, part)
+        return pltpu.make_async_remote_copy(
+            src_ref=held.at[rows_of(t, d, 0), columns],
+            dst_ref=held.at[rows_of(t + 1, d, 0), columns],
+            send_sem=ring_send.at[t, d, u],
+            recv_sem=ring_recv.at[t, d, u],
+            device_id={"blk": onward[d]},
+            device_id_type=pl.DeviceIdType.MESH,
+        )
+
+    def twin_copy(t, d, u):
+        columns = pl.ds(u * part, part)
+        return pltpu.make_async_remote_copy(
+            src_ref=held.at[rows_of(t, d, 0), columns],
+            dst_ref=held.at[rows_of(t, d, 1), columns],
+            send_sem=twin_send.at[t, d, u],
+            recv_sem=twin_recv.at[t, d, u],
+            device_id={"blk": twin},
+            device_id_type=pl.DeviceIdType.MESH,
+        )
+
+    def back_copy(t, d, k):
+        shift = t if d == 1 else chips - t
+        owner = device((place + shift) % chips, core if k == 0 else 1 - core)
+        return pltpu.make_async_remote_copy(
+            src_ref=stage.at[rows_of(t, d, k)],
+            dst_ref=out_ref.at[me, pl.ds(d * half, half)],
+            send_sem=back_send.at[t, d, k],
+            recv_sem=back_recv.at[t, d, k],
+            device_id={"blk": owner},
+            device_id_type=pl.DeviceIdType.MESH,
+        )
+
+    load = pltpu.make_async_copy(train_hbm, train, train_sem)
+    load.start()
+    barrier = pltpu.get_barrier_semaphore()
+
+    @pl.loop(1, blocks)
+    def _(k):
+        pl.semaphore_signal(
+            barrier, inc=1, device_id={"blk": (me + k) % blocks},
+            device_id_type=pl.DeviceIdType.MESH,
+        )
+
+    for d in range(2):
+        held[pl.ds(d * 2 * half, half), :] = x_ref[pl.ds(d * half, half), :]
+    pl.semaphore_wait(barrier, blocks - 1)
+
+    def multiply(g, q):
+        if q % (quanta // subs) == 0:
+            for step in range(2):
+                for d in range(2):
+                    twin_copy(g * 2 + step, d, q // (quanta // subs)).wait_recv()
+        columns = pl.ds(q * slice_of, slice_of)
+        base = pl.ds(pl.multiple_of(g * pair, pair), pair)
+        term = lax.dot_general(
+            held[base, columns], train[:, columns], (((1,), (1,)), ((), ())),
+            preferred_element_type=jnp.float32,
+        )
+        if q == 0:
+            total[...] = term
+        elif q < quanta - 1:
+            total[...] += term
+        else:
+            stage[base, :] = (total[...] + term).astype(jnp.bfloat16)
+            for step in range(2):
+                for d in range(2):
+                    for k in range(2):
+                        if step == 0 and k == 0:
+
+                            @pl.when(g > 0)
+                            def _():
+                                back_copy(g * 2 + step, d, k).start()
+
+                        else:
+                            back_copy(g * 2 + step, d, k).start()
+
+    @pl.loop(0, chips // 2)
+    def _(g):
+        for step in range(2):
+            t = g * 2 + step
+            for u in range(subs):
+                for d in range(2):
+                    if step == 0:
+
+                        @pl.when(g > 0)
+                        def _():
+                            ring_copy(t - 1, d, u).wait_recv()
+
+                    else:
+                        ring_copy(t - 1, d, u).wait_recv()
+                    if step == 1:
+
+                        @pl.when(g < chips // 2 - 1)
+                        def _():
+                            ring_copy(t, d, u).start()
+
+                    else:
+                        ring_copy(t, d, u).start()
+                    twin_copy(t, d, u).start()
+
+                @pl.when(g > 0)
+                def _():
+                    @pl.when(g == 1)
+                    def _():
+                        if step == 0 and u == 0:
+                            load.wait()
+
+                    multiply(g - 1, step * subs + u)
+
+    for q in range(quanta):
+        multiply(chips // 2 - 1, q)
+    for d in range(2):
+        out_ref[me, pl.ds(d * half, half), :] = stage[pl.ds(d * 2 * half, half), :]
+
+    @pl.loop(0, chips)
+    def _(t):
+        for d in range(2):
+            for u in range(subs):
+                twin_copy(t, d, u).wait_send()
+
+                @pl.when(t < chips - 1)
+                def _():
+                    ring_copy(t, d, u).wait_send()
+
+            back_copy(t, d, 1).wait()
+
+            @pl.when(t > 0)
+            def _():
+                back_copy(t, d, 0).wait()
+
+
+def ring_scores(conditioned, train_grads, blocks, cores):
+    rows, depth = conditioned.shape
+    count = train_grads.shape[0]
+    steps = blocks // cores
+    return pl.pallas_call(
+        functools.partial(ring_kernel, cores),
+        out_shape=jax.ShapeDtypeStruct((blocks, rows, count), jnp.bfloat16),
+        in_specs=[
+            pl.BlockSpec(memory_space=pltpu.VMEM),
+            pl.BlockSpec(memory_space=pl.ANY),
+        ],
+        out_specs=pl.BlockSpec(memory_space=pltpu.VMEM),
+        scratch_shapes=[
+            pltpu.VMEM((blocks * rows, depth), jnp.bfloat16),
+            pltpu.VMEM((count, depth), jnp.bfloat16),
+            pltpu.VMEM((4 * rows, count), jnp.float32),
+            pltpu.VMEM((blocks * rows, count), jnp.bfloat16),
+            pltpu.SemaphoreType.DMA,
+            pltpu.SemaphoreType.DMA((steps, 2, 2)),
+            pltpu.SemaphoreType.DMA((steps, 2, 2)),
+            pltpu.SemaphoreType.DMA((steps, 2, 2)),
+            pltpu.SemaphoreType.DMA((steps, 2, 2)),
+            pltpu.SemaphoreType.DMA((steps, 2, 2)),
+            pltpu.SemaphoreType.DMA((steps, 2, 2)),
+        ],
+        compiler_params=pltpu.CompilerParams(
+            collective_id=0, has_side_effects=True, vmem_limit_bytes=40 * 1024 * 1024
+        ),
+        name="ring_scores",
+    )(conditioned, train_grads)
+
+
+def plain_scores(conditioned, train_grads):
     scores = lax.dot_general(
         lax.all_gather(conditioned, "blk", axis=0, tiled=True),
         train_grads,
         (((1,), (1,)), ((), ())),
         preferred_element_type=jnp.float32,
     ).astype(jnp.bfloat16)
-    blocks = scores.shape[0] // queries.shape[0]
-    parted = lax.all_to_all(
-        scores.reshape(blocks, queries.shape[0], scores.shape[1]),
+    rows = conditioned.shape[0]
+    return lax.all_to_all(
+        scores.reshape(scores.shape[0] // rows, rows, scores.shape[1]),
         "blk",
         split_axis=0,
         concat_axis=0,
     )
+
+
+def local(blocks, queries, train_grads, group_of, basis_out, basis_in, eigen, store_ids):
+    conditioned = condition(queries, group_of, basis_out, basis_in, eigen)
+    if blocks == 16 and queries.shape[0] % 32 == 0:
+        parted = ring_scores(conditioned, train_grads, blocks, 2)
+    else:
+        parted = plain_scores(conditioned, train_grads)
     return arrange(parted, store_ids)
 
 
 def solution(mesh):
     return jax.shard_map(
-        local,
+        functools.partial(local, mesh.shape["blk"]),
         mesh=mesh,
         in_specs=(P("blk", None), P(("parts", "blk"), None), P(), P(), P(), P(), P("parts")),
         out_specs=P("blk", "parts"),

time: 146 us -> 91.6 us (0.63)
  waiting for transfers between devices: 77.8 us -> 0 us
  Pallas kernels: 21.2 us -> 82.2 us
  blocking collectives: 17.3 us -> 0 us
  between operations: 13.4 us -> 0.07 us
  matrix products: 10.3 us -> 0 us
  local copies, waits for them, and re-layouts: 4.69 us -> 8.07 us
    all_gather x1 -> x0, waiting for transfers between devices: 77.7 us -> none  [local(): lax.all_gather(conditioned, 'blk', axis=0, tiled=True)]
    pallas_call x0 -> x1, Pallas kernels: none -> 61.6 us  [ring_scores(): pl.pallas_call(functools.partial(ring_kernel, cores), out_shape=jax.Shape...]
    all_to_all x1 -> x0, blocking collectives: 17.3 us -> none  [local(): lax.all_to_all(scores.reshape(blocks, queries.shape[0], scores.shape[1]),...]
    dot_general x1 -> x0, matrix products: 10.3 us -> none  [local(): lax.dot_general(lax.all_gather(conditioned, 'blk', axis=0, tiled=True), t...]
    unnamed x8 -> x10, local copies, waits for them, and re-layouts: 3.7 us -> 7.07 us
  transfers between devices with their start and end apart: 1 -> 0, of which waited for: 1 -> 0; matrix products, arithmetic and copies ran while one was open for 0% -> 0% of each run, Pallas kernels for 0% -> 0%
where the time goes in v1:
time: 91.6 us; the launch traced here: 91.3 us
  Pallas kernels  82.2 us (90%)
  local copies, waits for them, and re-layouts  8.07 us (9%)
  other arithmetic  1.01 us (1%)
    pallas_call x1, Pallas kernels, ring_scores(): pl.pallas_call(functools.partial(ring_kernel, cores), out_shape=jax.Shape...  61.6 us
    pallas_call x1, Pallas kernels, arrange(): pl.pallas_call(arrange_kernel, grid=(blocks,), in_specs=[pl.BlockSpec((1,...  10.6 us
    pallas_call x1, Pallas kernels, condition(): pl.pallas_call(functools.partial(condition_kernel, order), grid_spec=pltp...  9.99 us
    unnamed x10, local copies, waits for them, and re-layouts  7.07 us

profile of v1, /device:TPU:0, one launch (start us, length us, event | category | flops | bytes accessed | tf_op | source)
XLA Modules:
  0.0 91.3 jit_solution(7124344129772592709)
XLA Ops:
  0.0 0.0 copy-start.2
  0.0 1.0 %reshape.6.eigen_ref = f32[8,8,128]{2,1,0:T(8,128)S(1)} reshape(f32[8,32,32]{2,1,0:T(8,128)} %param.12) | data formatting | bytes 65536 | tf_op jit(solution)/shard_map/reshape | solution.py:117
  1.0 1.0 %copy.13 = f32[8,32,32]{1,2,0:T(8,128)S(1)} copy(f32[8,32,32]{2,1,0:T(8,128)} %param.10) | data formatting | bytes 65536 | tf_op args[3]
  2.0 1.0 %copy.14 = f32[8,32,32]{1,2,0:T(8,128)S(1)} copy(f32[8,32,32]{2,1,0:T(8,128)} %param.11) | data formatting | bytes 65536 | tf_op args[4]
  3.0 1.0 %pad_maximum_fusion.bases_ref = f32[8,128,32]{2,1,0:T(8,128)S(1)} fusion(f32[8,32,32]{2,1,0:T(8,128)S(1)} %bitcast.5, f32[8,32,32]{2,1,0:T(8,128)} %param.11, f32[8,32,32]{2,1,0:T(8,128)S(1)} %bitcast.4, f32[8,32,32]{2,1,0:T(8,128)} %param.10), kind=kLoop, calls=%fused_computation | loop fusion | flops 98304 | bytes 262144 | tf_op jit(solution)/shard_map/concatenate | solution.py:98
  4.0 0.0 copy-start.1
  4.0 1.0 %copy-done.1 = bf16[32,8192]{1,0:T(8,128)(2,1)S(1)} copy-done((bf16[32,8192]{1,0:T(8,128)(2,1)S(1)}, bf16[32,8192]{1,0:T(8,128)(2,1)}, u32[]{:S(2)}) %copy-start.1) | copy-done | bytes 524312
  5.1 0.0 copy-start.3
  5.1 0.7 copy-done.3
  5.7 10.0 %condition.1.x_ref = bf16[32,8192]{1,0:T(8,128)(2,1)S(1)} custom-call(s32[8]{0:T(128)S(1)} %copy-done.3, bf16[32,8192]{1,0:T(8,128)(2,1)S(1)} %copy-done.1, f32[8,128,32]{2,1,0:T(8,128)S(1)} %pad_maximum_fusion.bases_ref, f32[8,8,128]{2,1,0:T(8,128)S(1)} %reshape.6.eigen_ref), custom_call_target="tpu_custom_call" | custom-call | tf_op jit(solution)/shard_map/condition/pallas_call | solution.py:102
  15.7 0.0 copy-start
  15.8 3.4 %copy-done = bf16[512,8192]{1,0:T(8,128)(2,1)S(1)} copy-done((bf16[512,8192]{1,0:T(8,128)(2,1)S(1)}, bf16[512,8192]{1,0:T(8,128)(2,1)}, u32[]{:S(2)}) %copy-start) | copy-done | bytes 8388632
  19.1 61.6 %ring_scores.1.scores_ref = bf16[16,32,512]{2,1,0:T(8,128)(2,1)S(1)} custom-call(bf16[32,8192]{1,0:T(8,128)(2,1)S(1)} %condition.1.x_ref, bf16[512,8192]{1,0:T(8,128)(2,1)S(1)} %copy-done), custom_call_target="tpu_custom_call" | custom-call | tf_op jit(solution)/shard_map/ring_scores/pallas_call | solution.py:338
  80.7 0.0 copy-done.2
  80.7 10.6 %arrange.1 = bf16[32,8192]{1,0:T(8,128)(2,1)} custom-call(bf16[16,32,512]{2,1,0:T(8,128)(2,1)S(1)} %ring_scores.1.scores_ref, s32[16,1,512]{2,1,0:T(1,128)S(1)} %bitcast.3), custom_call_target="tpu_custom_call" | custom-call | tf_op jit(solution)/shard_map/arrange/pallas_call | solution.py:156
Async XLA Ops:
  0.0 80.7 %copy-start.2 = (s32[8192]{0:T(1024)S(1)}, s32[8192]{0:T(1024)}, u32[]{:S(2)}) copy-start(s32[8192]{0:T(1024)} %param.13) | copy-start | bytes 98308
  4.0 1.0 %copy-start.1 = (bf16[32,8192]{1,0:T(8,128)(2,1)S(1)}, bf16[32,8192]{1,0:T(8,128)(2,1)}, u32[]{:S(2)}) copy-start(bf16[32,8192]{1,0:T(8,128)(2,1)} %x_ref.1) | copy-start | bytes 1572868
  5.1 0.7 copy-start.3
  15.7 3.4 %copy-start = (bf16[512,8192]{1,0:T(8,128)(2,1)S(1)}, bf16[512,8192]{1,0:T(8,128)(2,1)}, u32[]{:S(2)}) copy-start(bf16[512,8192]{1,0:T(8,128)(2,1)} %train_hbm.1) | copy-start | bytes 25165828

commit v2 on v1

--- a/solution.py
+++ b/solution.py
@@ -119,16 +119,18 @@
 
 def arrange_kernel(scores_ref, ids_ref, out_ref, total):
     step = pl.program_id(0)
-    rows, count = scores_ref.shape[1:]
+    taken, rows, count = scores_ref.shape
     groups = out_ref.shape[1] // WIDE
-    ids = ids_ref[0]
+    ids = jnp.concatenate([ids_ref[k] for k in range(taken)], axis=1)
     coarse = ids // WIDE
     fine = ids % WIDE
-    scores = scores_ref[0].astype(jnp.float32)
+    scores = jnp.concatenate([scores_ref[k] for k in range(taken)], axis=1).astype(
+        jnp.float32
+    )
     left = jnp.concatenate(
         [jnp.where(coarse == h, scores, 0.0) for h in range(groups)], axis=0
     ).astype(jnp.bfloat16)
-    line = lax.broadcasted_iota(jnp.int32, (WIDE, count), 0)
+    line = lax.broadcasted_iota(jnp.int32, (WIDE, taken * count), 0)
     chosen = jnp.where(line == fine, 1.0, 0.0).astype(jnp.bfloat16)
     term = lax.dot_general(
         left, chosen, (((1,), (1,)), ((), ())), preferred_element_type=jnp.float32
@@ -153,12 +155,13 @@
 def arrange(parted, ids):
     blocks, rows, count = parted.shape
     width = blocks * count
+    taken = 4 if blocks % 4 == 0 else 1
     return pl.pallas_call(
         arrange_kernel,
-        grid=(blocks,),
+        grid=(blocks // taken,),
         in_specs=[
-            pl.BlockSpec((1, rows, count), lambda k: (k, 0, 0)),
-            pl.BlockSpec((1, 1, count), lambda k: (k, 0, 0)),
+            pl.BlockSpec((taken, rows, count), lambda k: (k, 0, 0)),
+            pl.BlockSpec((taken, 1, count), lambda k: (k, 0, 0)),
         ],
         out_specs=pl.BlockSpec((rows, width), lambda k: (0, 0)),
         out_shape=jax.ShapeDtypeStruct((rows, width), jnp.bfloat16),
@@ -169,16 +172,15 @@
 
 
 def ring_kernel(cores, x_ref, train_hbm, out_ref, held, train, total, stage, train_sem,
-                ring_send, ring_recv, twin_send, twin_recv, back_send, back_recv):
+                ring_send, ring_recv, twin_send, twin_recv, back_send, back_recv,
+                side_send, side_recv):
     blocks, rows, count = out_ref.shape
     half = rows // 2
     depth = x_ref.shape[1]
     chips = blocks // cores
     long = chips // 2
-    subs = 2
-    part = depth // subs
-    quanta = 4
-    slice_of = depth // quanta
+    third = (depth // 3 + WIDE // 2) // WIDE * WIDE
+    slab = lax.axis_index("parts")
     step_rows = 4 * half
     pair = 2 * step_rows
     me = lax.axis_index("blk")
@@ -195,11 +197,17 @@
     onward = [device((place + 1) % chips, core), device((place + chips - 1) % chips, core)]
     twin = device(place, 1 - core)
 
+    def columns_of(u):
+        if u == 1:
+            return pl.ds(2 * third, depth - 2 * third)
+        start = slab if u == 0 else 1 - slab
+        return pl.ds(pl.multiple_of(start * third, WIDE), third)
+
     def rows_of(t, d, k):
         return pl.ds(pl.multiple_of((t * 4 + d * 2 + k) * half, half), half)
 
     def ring_copy(t, d, u):
-        columns = pl.ds(u * part, part)
+        columns = columns_of(u)
         return pltpu.make_async_remote_copy(
             src_ref=held.at[rows_of(t, d, 0), columns],
             dst_ref=held.at[rows_of(t + 1, d, 0), columns],
@@ -210,13 +218,24 @@
         )
 
     def twin_copy(t, d, u):
-        columns = pl.ds(u * part, part)
+        columns = columns_of(u)
         return pltpu.make_async_remote_copy(
             src_ref=held.at[rows_of(t, d, 0), columns],
             dst_ref=held.at[rows_of(t, d, 1), columns],
             send_sem=twin_send.at[t, d, u],
             recv_sem=twin_recv.at[t, d, u],
             device_id={"blk": twin},
+            device_id_type=pl.DeviceIdType.MESH,
+        )
+
+    def side_copy(t, d):
+        columns = columns_of(0)
+        return pltpu.make_async_remote_copy(
+            src_ref=held.at[rows_of(t, d, 0), columns],
+            dst_ref=held.at[rows_of(t, d, 0), columns],
+            send_sem=side_send.at[t, d],
+            recv_sem=side_recv.at[t, d],
+            device_id={"parts": 1 - slab},
             device_id_type=pl.DeviceIdType.MESH,
         )
 
@@ -243,16 +262,19 @@
             device_id_type=pl.DeviceIdType.MESH,
         )
 
+    pl.semaphore_signal(
+        barrier, inc=1, device_id={"parts": 1 - slab},
+        device_id_type=pl.DeviceIdType.MESH,
+    )
     for d in range(2):
         held[pl.ds(d * 2 * half, half), :] = x_ref[pl.ds(d * half, half), :]
-    pl.semaphore_wait(barrier, blocks - 1)
+    pl.semaphore_wait(barrier, blocks)
 
     def multiply(g, q):
-        if q % (quanta // subs) == 0:
-            for step in range(2):
-                for d in range(2):
-                    twin_copy(g * 2 + step, d, q // (quanta // subs)).wait_recv()
-        columns = pl.ds(q * slice_of, slice_of)
+        for step in range(2):
+            for d in range(2):
+                twin_copy(g * 2 + step, d, q).wait_recv()
+        columns = columns_of(q)
         base = pl.ds(pl.multiple_of(g * pair, pair), pair)
         term = lax.dot_general(
             held[base, columns], train[:, columns], (((1,), (1,)), ((), ())),
@@ -260,7 +282,7 @@
         )
         if q == 0:
             total[...] = term
-        elif q < quanta - 1:
+        elif q == 1:
             total[...] += term
         else:
             stage[base, :] = (total[...] + term).astype(jnp.bfloat16)
@@ -276,11 +298,21 @@
                         else:
                             back_copy(g * 2 + step, d, k).start()
 
+    def from_side(t):
+        for d in range(2):
+            side_copy(t, d).wait_recv()
+            twin_copy(t, d, 2).start()
+
+    def forward(t, d, u):
+        ring_copy(t, d, u).start()
+
+    last = chips // 2 - 1
+
     @pl.loop(0, chips // 2)
     def _(g):
         for step in range(2):
             t = g * 2 + step
-            for u in range(subs):
+            for u in range(2):
                 for d in range(2):
                     if step == 0:
 
@@ -288,37 +320,72 @@
                         def _():
                             ring_copy(t - 1, d, u).wait_recv()
 
+                        forward(t, d, u)
                     else:
                         ring_copy(t - 1, d, u).wait_recv()
-                    if step == 1:
-
-                        @pl.when(g < chips // 2 - 1)
+
+                        @pl.when(g < last)
                         def _():
-                            ring_copy(t, d, u).start()
-
-                    else:
-                        ring_copy(t, d, u).start()
+                            forward(t, d, u)
+
+                    if u == 0:
+                        if step == 0:
+
+                            @pl.when(g > 0)
+                            def _():
+                                side_copy(t, d).start()
+
+                        else:
+                            side_copy(t, d).start()
                     twin_copy(t, d, u).start()
+                if step == 0:
+
+                    @pl.when(g > 0)
+                    def _():
+                        if u == 0:
+
+                            @pl.when(g == 1)
+                            def _():
+                                load.wait()
+
+                        multiply(g - 1, u)
+
+                elif u == 0:
+
+                    @pl.when(g > 0)
+                    def _():
+                        multiply(g - 1, 2)
+
+            if step == 0:
+
+                @pl.when(g == 0)
+                def _():
+                    for d in range(2):
+                        twin_copy(t, d, 2).start()
 
                 @pl.when(g > 0)
                 def _():
-                    @pl.when(g == 1)
-                    def _():
-                        if step == 0 and u == 0:
-                            load.wait()
-
-                    multiply(g - 1, step * subs + u)
-
-    for q in range(quanta):
-        multiply(chips // 2 - 1, q)
+                    from_side(t - 1)
+
+            else:
+
+                @pl.when(g > 0)
+                def _():
+                    from_side(t - 1)
+
+    multiply(last, 0)
+    multiply(last, 1)
+    from_side(chips - 1)
+    multiply(last, 2)
     for d in range(2):
         out_ref[me, pl.ds(d * half, half), :] = stage[pl.ds(d * 2 * half, half), :]
 
     @pl.loop(0, chips)
     def _(t):
         for d in range(2):
-            for u in range(subs):
+            for u in range(3):
                 twin_copy(t, d, u).wait_send()
+            for u in range(2):
 
                 @pl.when(t < chips - 1)
                 def _():
@@ -328,6 +395,7 @@
 
             @pl.when(t > 0)
             def _():
+                side_copy(t, d).wait_send()
                 back_copy(t, d, 0).wait()
 
 
@@ -351,13 +419,15 @@
             pltpu.SemaphoreType.DMA,
             pltpu.SemaphoreType.DMA((steps, 2, 2)),
             pltpu.SemaphoreType.DMA((steps, 2, 2)),
+            pltpu.SemaphoreType.DMA((steps, 2, 3)),
+            pltpu.SemaphoreType.DMA((steps, 2, 3)),
             pltpu.SemaphoreType.DMA((steps, 2, 2)),
             pltpu.SemaphoreType.DMA((steps, 2, 2)),
-            pltpu.SemaphoreType.DMA((steps, 2, 2)),
-            pltpu.SemaphoreType.DMA((steps, 2, 2)),
+            pltpu.SemaphoreType.DMA((steps, 2)),
+            pltpu.SemaphoreType.DMA((steps, 2)),
         ],
         compiler_params=pltpu.CompilerParams(
-            collective_id=0, has_side_effects=True, vmem_limit_bytes=40 * 1024 * 1024
+            collective_id=0, has_side_effects=True, vmem_limit_bytes=56 * 1024 * 1024
         ),
         name="ring_scores",
     )(conditioned, train_grads)
@@ -379,9 +449,9 @@
     )
 
 
-def local(blocks, queries, train_grads, group_of, basis_out, basis_in, eigen, store_ids):
+def local(parts, blocks, queries, train_grads, group_of, basis_out, basis_in, eigen, store_ids):
     conditioned = condition(queries, group_of, basis_out, basis_in, eigen)
-    if blocks == 16 and queries.shape[0] % 32 == 0:
+    if parts == 2 and blocks == 16 and queries.shape[0] % 32 == 0:
         parted = ring_scores(conditioned, train_grads, blocks, 2)
     else:
         parted = plain_scores(conditioned, train_grads)
@@ -390,7 +460,7 @@
 
 def solution(mesh):
     return jax.shard_map(
-        functools.partial(local, mesh.shape["blk"]),
+        functools.partial(local, mesh.shape["parts"], mesh.shape["blk"]),
         mesh=mesh,
         in_specs=(P("blk", None), P(("parts", "blk"), None), P(), P(), P(), P(), P("parts")),
         out_specs=P("blk", "parts"),

time: 91.6 us -> 78.6 us (0.86)
  Pallas kernels: 82.2 us -> 70.7 us
  local copies, waits for them, and re-layouts: 8.07 us -> 6.51 us
    pallas_call x1, Pallas kernels: 61.6 us -> 54.3 us  [ring_scores(): pl.pallas_call(functools.partial(ring_kernel, cores), out_shape=jax.Shape...]
    pallas_call x1, Pallas kernels: 10.6 us -> 6.42 us  [arrange(): pl.pallas_call(arrange_kernel, grid=(blocks // taken,), in_specs=[pl.Bloc...]
    unnamed x10 -> x12, local copies, waits for them, and re-layouts: 7.07 us -> 5.52 us
where the time goes in v2:
time: 78.6 us; the launch traced here: 78.3 us
  Pallas kernels  70.7 us (90%)
  local copies, waits for them, and re-layouts  6.51 us (8%)
  other arithmetic  1.01 us (1%)
    pallas_call x1, Pallas kernels, ring_scores(): pl.pallas_call(functools.partial(ring_kernel, cores), out_shape=jax.Shape...  54.3 us
    pallas_call x1, Pallas kernels, condition(): pl.pallas_call(functools.partial(condition_kernel, order), grid_spec=pltp...  9.99 us
    pallas_call x1, Pallas kernels, arrange(): pl.pallas_call(arrange_kernel, grid=(blocks // taken,), in_specs=[pl.Bloc...  6.42 us
    unnamed x12, local copies, waits for them, and re-layouts  5.52 us

profile of v2, /device:TPU:0, one launch (start us, length us, event | category | flops | bytes accessed | tf_op | source)
XLA Modules:
  0.0 78.3 jit_solution(6058417366794355102)
XLA Ops:
  0.0 0.0 copy-start.3
  0.0 1.0 %reshape.6.eigen_ref = f32[8,8,128]{2,1,0:T(8,128)S(1)} reshape(f32[8,32,32]{2,1,0:T(8,128)} %param.12) | data formatting | bytes 65536 | tf_op jit(solution)/shard_map/reshape | solution.py:117
  1.0 1.0 %copy.13 = f32[8,32,32]{1,2,0:T(8,128)S(1)} copy(f32[8,32,32]{2,1,0:T(8,128)} %param.10) | data formatting | bytes 65536 | tf_op args[3]
  2.0 1.0 %copy.14 = f32[8,32,32]{1,2,0:T(8,128)S(1)} copy(f32[8,32,32]{2,1,0:T(8,128)} %param.11) | data formatting | bytes 65536 | tf_op args[4]
  3.0 1.0 %pad_maximum_fusion.bases_ref = f32[8,128,32]{2,1,0:T(8,128)S(1)} fusion(f32[8,32,32]{2,1,0:T(8,128)S(1)} %bitcast.5, f32[8,32,32]{2,1,0:T(8,128)} %param.11, f32[8,32,32]{2,1,0:T(8,128)S(1)} %bitcast.4, f32[8,32,32]{2,1,0:T(8,128)} %param.10), kind=kLoop, calls=%fused_computation | loop fusion | flops 98304 | bytes 262144 | tf_op jit(solution)/shard_map/concatenate | solution.py:98
  4.0 0.0 copy-start.2
  4.0 1.0 %copy-done.2 = bf16[32,8192]{1,0:T(8,128)(2,1)S(1)} copy-done((bf16[32,8192]{1,0:T(8,128)(2,1)S(1)}, bf16[32,8192]{1,0:T(8,128)(2,1)}, u32[]{:S(2)}) %copy-start.2) | copy-done | bytes 524312
  5.1 0.0 copy-start.4
  5.1 0.7 copy-done.4
  5.7 10.0 %condition.1.x_ref = bf16[32,8192]{1,0:T(8,128)(2,1)S(1)} custom-call(s32[8]{0:T(128)S(1)} %copy-done.4, bf16[32,8192]{1,0:T(8,128)(2,1)S(1)} %copy-done.2, f32[8,128,32]{2,1,0:T(8,128)S(1)} %pad_maximum_fusion.bases_ref, f32[8,8,128]{2,1,0:T(8,128)S(1)} %reshape.6.eigen_ref), custom_call_target="tpu_custom_call" | custom-call | tf_op jit(solution)/shard_map/condition/pallas_call | solution.py:102
  15.7 0.0 copy-start
  15.8 0.8 %copy-done = bf16[32,8192]{1,0:T(8,128)(2,1)} copy-done((bf16[32,8192]{1,0:T(8,128)(2,1)}, bf16[32,8192]{1,0:T(8,128)(2,1)S(1)}, u32[]{:S(2)}) %copy-start) | copy-done | bytes 524312
  16.5 54.3 %ring_scores.1.scores_ref = bf16[16,32,512]{2,1,0:T(8,128)(2,1)} custom-call(bf16[32,8192]{1,0:T(8,128)(2,1)} %copy-done, bf16[512,8192]{1,0:T(8,128)(2,1)} %train_hbm.1), custom_call_target="tpu_custom_call" | custom-call | tf_op jit(solution)/shard_map/ring_scores/pallas_call | solution.py:406
  70.8 0.0 copy-done.3
  70.8 0.0 copy-start.1
  70.9 1.0 %copy-done.1 = bf16[16,32,512]{2,1,0:T(8,128)(2,1)S(1)} copy-done((bf16[16,32,512]{2,1,0:T(8,128)(2,1)S(1)}, bf16[16,32,512]{2,1,0:T(8,128)(2,1)}, u32[]{:S(2)}) %copy-start.1) | copy-done | bytes 524312
  71.9 6.4 %arrange.1 = bf16[32,8192]{1,0:T(8,128)(2,1)} custom-call(bf16[16,32,512]{2,1,0:T(8,128)(2,1)S(1)} %copy-done.1, s32[16,1,512]{2,1,0:T(1,128)S(1)} %bitcast.3), custom_call_target="tpu_custom_call" | custom-call | tf_op jit(solution)/shard_map/arrange/pallas_call | solution.py:159
Async XLA Ops:
  0.0 70.8 %copy-start.3 = (s32[8192]{0:T(1024)S(1)}, s32[8192]{0:T(1024)}, u32[]{:S(2)}) copy-start(s32[8192]{0:T(1024)} %param.13) | copy-start | bytes 98308
  4.0 1.0 %copy-start.2 = (bf16[32,8192]{1,0:T(8,128)(2,1)S(1)}, bf16[32,8192]{1,0:T(8,128)(2,1)}, u32[]{:S(2)}) copy-start(bf16[32,8192]{1,0:T(8,128)(2,1)} %x_ref.1) | copy-start | bytes 1572868
  5.1 0.7 copy-start.4
  15.7 0.8 %copy-start = (bf16[32,8192]{1,0:T(8,128)(2,1)}, bf16[32,8192]{1,0:T(8,128)(2,1)S(1)}, u32[]{:S(2)}) copy-start(bf16[32,8192]{1,0:T(8,128)(2,1)S(1)} %condition.1.x_ref) | copy-start | bytes 1572868
  70.8 1.0 %copy-start.1 = (bf16[16,32,512]{2,1,0:T(8,128)(2,1)S(1)}, bf16[16,32,512]{2,1,0:T(8,128)(2,1)}, u32[]{:S(2)}) copy-start(bf16[16,32,512]{2,1,0:T(8,128)(2,1)} %ring_scores.1.scores_ref) | copy-start | bytes 1572868

commit v3 on v2

--- a/solution.py
+++ b/solution.py
@@ -27,12 +27,13 @@
     )
 
 
-def condition_kernel(order, group_ref, x_ref, bases_ref, eigen_ref, out_ref):
+def condition_kernel(order, group_ref, x_ref, output_ref, input_ref, eigen_ref, out_ref):
     del group_ref
     rows = x_ref.shape[0]
     per = LANES // order
     chunks = order // per
-    bases = bases_ref[0]
+    output, inputs = output_ref[0], input_ref[0]
+    bases = jnp.concatenate([output, output.T, inputs, inputs.T], axis=0)
     lane = lax.broadcasted_iota(jnp.int32, (order, order * order), 1)
     line = lax.broadcasted_iota(jnp.int32, (order, order * order), 0)
     spread = jnp.where(lane // order == line, 1.0, 0.0).astype(jnp.bfloat16)
@@ -95,10 +96,6 @@
     groups, order, _ = eigen.shape
     rows = queries.shape[0]
     size = order * order
-    bases = jnp.concatenate(
-        [basis_out, jnp.swapaxes(basis_out, 1, 2), basis_in, jnp.swapaxes(basis_in, 1, 2)],
-        axis=1,
-    )
     return pl.pallas_call(
         functools.partial(condition_kernel, order),
         grid_spec=pltpu.PrefetchScalarGridSpec(
@@ -106,7 +103,8 @@
             grid=(groups,),
             in_specs=[
                 pl.BlockSpec((rows, size), lambda b, g: (0, b)),
-                pl.BlockSpec((1, 4 * order, order), lambda b, g: (g[b], 0, 0)),
+                pl.BlockSpec((1, order, order), lambda b, g: (g[b], 0, 0)),
+                pl.BlockSpec((1, order, order), lambda b, g: (g[b], 0, 0)),
                 pl.BlockSpec((1, size // LANES, LANES), lambda b, g: (g[b], 0, 0)),
             ],
             out_specs=pl.BlockSpec((rows, size), lambda b, g: (0, b)),
@@ -114,7 +112,7 @@
         out_shape=jax.ShapeDtypeStruct(queries.shape, jnp.bfloat16),
         compiler_params=pltpu.CompilerParams(vmem_limit_bytes=32 * 1024 * 1024),
         name="condition",
-    )(group_of, queries, bases, eigen.reshape(groups, size // LANES, LANES))
+    )(group_of, queries, basis_out, basis_in, eigen.reshape(groups, size // LANES, LANES))
 
 
 def arrange_kernel(scores_ref, ids_ref, out_ref, total):
@@ -197,17 +195,26 @@
     onward = [device((place + 1) % chips, core), device((place + chips - 1) % chips, core)]
     twin = device(place, 1 - core)
 
-    def columns_of(u):
-        if u == 1:
+    def columns_of(q):
+        if q == 1:
             return pl.ds(2 * third, depth - 2 * third)
-        start = slab if u == 0 else 1 - slab
+        start = slab if q == 0 else 1 - slab
         return pl.ds(pl.multiple_of(start * third, WIDE), third)
+
+    def piece_of(u):
+        if u == 4:
+            return columns_of(2)
+        if u < 2:
+            size = third // 2
+            return pl.ds(pl.multiple_of(slab * third + u * size, LANES), size)
+        size = (depth - 2 * third) // 2
+        return pl.ds(2 * third + (u - 2) * size, size)
 
     def rows_of(t, d, k):
         return pl.ds(pl.multiple_of((t * 4 + d * 2 + k) * half, half), half)
 
     def ring_copy(t, d, u):
-        columns = columns_of(u)
+        columns = piece_of(u)
         return pltpu.make_async_remote_copy(
             src_ref=held.at[rows_of(t, d, 0), columns],
             dst_ref=held.at[rows_of(t + 1, d, 0), columns],
@@ -218,7 +225,7 @@
         )
 
     def twin_copy(t, d, u):
-        columns = columns_of(u)
+        columns = piece_of(u)
         return pltpu.make_async_remote_copy(
             src_ref=held.at[rows_of(t, d, 0), columns],
             dst_ref=held.at[rows_of(t, d, 1), columns],
@@ -270,22 +277,27 @@
         held[pl.ds(d * 2 * half, half), :] = x_ref[pl.ds(d * half, half), :]
     pl.semaphore_wait(barrier, blocks)
 
-    def multiply(g, q):
-        for step in range(2):
-            for d in range(2):
-                twin_copy(g * 2 + step, d, q).wait_recv()
+    def multiply(g, q, n):
+        if n == 0:
+            for step in range(2):
+                for d in range(2):
+                    for u in ((0, 1), (2, 3), (4,))[q]:
+                        twin_copy(g * 2 + step, d, u).wait_recv()
         columns = columns_of(q)
         base = pl.ds(pl.multiple_of(g * pair, pair), pair)
+        width = count // 2
         term = lax.dot_general(
-            held[base, columns], train[:, columns], (((1,), (1,)), ((), ())),
-            preferred_element_type=jnp.float32,
-        )
+            held[base, columns], train[n * width : (n + 1) * width, columns],
+            (((1,), (1,)), ((), ())), preferred_element_type=jnp.float32,
+        )
+        sums = pl.ds(n * width, width)
         if q == 0:
-            total[...] = term
+            total[:, sums] = term
         elif q == 1:
-            total[...] += term
+            total[:, sums] += term
         else:
-            stage[base, :] = (total[...] + term).astype(jnp.bfloat16)
+            stage[base, sums] = (total[:, sums] + term).astype(jnp.bfloat16)
+        if q == 2 and n == 1:
             for step in range(2):
                 for d in range(2):
                     for k in range(2):
@@ -301,7 +313,7 @@
     def from_side(t):
         for d in range(2):
             side_copy(t, d).wait_recv()
-            twin_copy(t, d, 2).start()
+            twin_copy(t, d, 4).start()
 
     def forward(t, d, u):
         ring_copy(t, d, u).start()
@@ -312,7 +324,7 @@
     def _(g):
         for step in range(2):
             t = g * 2 + step
-            for u in range(2):
+            for u in range(4):
                 for d in range(2):
                     if step == 0:
 
@@ -328,7 +340,7 @@
                         def _():
                             forward(t, d, u)
 
-                    if u == 0:
+                    if u == 1:
                         if step == 0:
 
                             @pl.when(g > 0)
@@ -348,20 +360,20 @@
                             def _():
                                 load.wait()
 
-                        multiply(g - 1, u)
-
-                elif u == 0:
+                        multiply(g - 1, u // 2, u % 2)
+
+                elif u < 2:
 
                     @pl.when(g > 0)
                     def _():
-                        multiply(g - 1, 2)
+                        multiply(g - 1, 2, u)
 
             if step == 0:
 
                 @pl.when(g == 0)
                 def _():
                     for d in range(2):
-                        twin_copy(t, d, 2).start()
+                        twin_copy(t, d, 4).start()
 
                 @pl.when(g > 0)
                 def _():
@@ -373,19 +385,20 @@
                 def _():
                     from_side(t - 1)
 
-    multiply(last, 0)
-    multiply(last, 1)
+    for u in range(4):
+        multiply(last, u // 2, u % 2)
     from_side(chips - 1)
-    multiply(last, 2)
+    for n in range(2):
+        multiply(last, 2, n)
     for d in range(2):
         out_ref[me, pl.ds(d * half, half), :] = stage[pl.ds(d * 2 * half, half), :]
 
     @pl.loop(0, chips)
     def _(t):
         for d in range(2):
-            for u in range(3):
+            for u in range(5):
                 twin_copy(t, d, u).wait_send()
-            for u in range(2):
+            for u in range(4):
 
                 @pl.when(t < chips - 1)
                 def _():
@@ -417,10 +430,10 @@
             pltpu.VMEM((4 * rows, count), jnp.float32),
             pltpu.VMEM((blocks * rows, count), jnp.bfloat16),
             pltpu.SemaphoreType.DMA,
-            pltpu.SemaphoreType.DMA((steps, 2, 2)),
-            pltpu.SemaphoreType.DMA((steps, 2, 2)),
-            pltpu.SemaphoreType.DMA((steps, 2, 3)),
-            pltpu.SemaphoreType.DMA((steps, 2, 3)),
+            pltpu.SemaphoreType.DMA((steps, 2, 4)),
+            pltpu.SemaphoreType.DMA((steps, 2, 4)),
+            pltpu.SemaphoreType.DMA((steps, 2, 5)),
+            pltpu.SemaphoreType.DMA((steps, 2, 5)),
             pltpu.SemaphoreType.DMA((steps, 2, 2)),
             pltpu.SemaphoreType.DMA((steps, 2, 2)),
             pltpu.SemaphoreType.DMA((steps, 2)),

time: 78.6 us -> 78.3 us (level)
  other arithmetic: 1.01 us -> 0 us
  Pallas kernels: 70.7 us -> 71.6 us
    concatenate x1 -> x0, other arithmetic: 1.01 us -> none  [condition(): jnp.concatenate([basis_out, jnp.swapaxes(basis_out, 1, 2), basis_in, jnp....]
    unnamed x12 -> x14, local copies, waits for them, and re-layouts: 5.52 us -> 5.33 us
where the time goes in v3:
time: 78.3 us; the launch traced here: 78 us
  Pallas kernels  71.6 us (91%)
  local copies, waits for them, and re-layouts  6.32 us (8%)
    pallas_call x1, Pallas kernels, ring_scores(): pl.pallas_call(functools.partial(ring_kernel, cores), out_shape=jax.Shape...  54.7 us
    pallas_call x1, Pallas kernels, condition(): pl.pallas_call(functools.partial(condition_kernel, order), grid_spec=pltp...  10.5 us
    pallas_call x1, Pallas kernels, arrange(): pl.pallas_call(arrange_kernel, grid=(blocks // taken,), in_specs=[pl.Bloc...  6.41 us
    unnamed x14, local copies, waits for them, and re-layouts  5.33 us

profile of v3, /device:TPU:0, one launch (start us, length us, event | category | flops | bytes accessed | tf_op | source)
XLA Modules:
  0.0 78.0 jit_solution(6561513142114048759)
XLA Ops:
  0.0 0.0 copy-start.5
  0.0 1.0 %reshape.6.eigen_ref = f32[8,8,128]{2,1,0:T(8,128)S(1)} reshape(f32[8,32,32]{2,1,0:T(8,128)} %param.12) | data formatting | bytes 65536 | tf_op jit(solution)/shard_map/reshape | solution.py:115
  1.0 0.0 copy-start.2
  1.0 1.0 %copy-done.2 = bf16[32,8192]{1,0:T(8,128)(2,1)S(1)} copy-done((bf16[32,8192]{1,0:T(8,128)(2,1)S(1)}, bf16[32,8192]{1,0:T(8,128)(2,1)}, u32[]{:S(2)}) %copy-start.2) | copy-done | bytes 524312
  2.1 0.0 copy-start.3
  2.1 0.9 %copy-done.3 = f32[8,32,32]{2,1,0:T(8,128)S(1)} copy-done((f32[8,32,32]{2,1,0:T(8,128)S(1)}, f32[8,32,32]{2,1,0:T(8,128)}, u32[]{:S(2)}) %copy-start.3) | copy-done | bytes 32792
  3.0 0.0 copy-start.4
  3.0 0.9 %copy-done.4 = f32[8,32,32]{2,1,0:T(8,128)S(1)} copy-done((f32[8,32,32]{2,1,0:T(8,128)S(1)}, f32[8,32,32]{2,1,0:T(8,128)}, u32[]{:S(2)}) %copy-start.4) | copy-done | bytes 32792
  3.9 0.0 copy-start.6
  3.9 0.7 copy-done.6
  4.5 10.5 %condition.1.x_ref = bf16[32,8192]{1,0:T(8,128)(2,1)S(1)} custom-call(s32[8]{0:T(128)S(1)} %copy-done.6, bf16[32,8192]{1,0:T(8,128)(2,1)S(1)} %copy-done.2, f32[8,32,32]{2,1,0:T(8,128)S(1)} %copy-done.3, f32[8,32,32]{2,1,0:T(8,128)S(1)} %copy-done.4, f32[8,8,128]{2,1,0:T(8,128)S(1)} %reshape.6.eigen_ref), custom_call_target="tpu_custom_call" | custom-call | tf_op jit(solution)/shard_map/condition/pallas_call | solution.py:99
  15.1 0.0 copy-start
  15.1 0.8 %copy-done = bf16[32,8192]{1,0:T(8,128)(2,1)} copy-done((bf16[32,8192]{1,0:T(8,128)(2,1)}, bf16[32,8192]{1,0:T(8,128)(2,1)S(1)}, u32[]{:S(2)}) %copy-start) | copy-done | bytes 524312
  15.8 54.7 %ring_scores.1.scores_ref = bf16[16,32,512]{2,1,0:T(8,128)(2,1)} custom-call(bf16[32,8192]{1,0:T(8,128)(2,1)} %copy-done, bf16[512,8192]{1,0:T(8,128)(2,1)} %train_hbm.1), custom_call_target="tpu_custom_call" | custom-call | tf_op jit(solution)/shard_map/ring_scores/pallas_call | solution.py:419
  70.5 0.0 copy-done.5
  70.5 0.0 copy-start.1
  70.6 1.0 %copy-done.1 = bf16[16,32,512]{2,1,0:T(8,128)(2,1)S(1)} copy-done((bf16[16,32,512]{2,1,0:T(8,128)(2,1)S(1)}, bf16[16,32,512]{2,1,0:T(8,128)(2,1)}, u32[]{:S(2)}) %copy-start.1) | copy-done | bytes 524312
  71.6 6.4 %arrange.1 = bf16[32,8192]{1,0:T(8,128)(2,1)} custom-call(bf16[16,32,512]{2,1,0:T(8,128)(2,1)S(1)} %copy-done.1, s32[16,1,512]{2,1,0:T(1,128)S(1)} %bitcast.1), custom_call_target="tpu_custom_call" | custom-call | tf_op jit(solution)/shard_map/arrange/pallas_call | solution.py:157
Async XLA Ops:
  0.0 70.5 %copy-start.5 = (s32[8192]{0:T(1024)S(1)}, s32[8192]{0:T(1024)}, u32[]{:S(2)}) copy-start(s32[8192]{0:T(1024)} %param.13) | copy-start | bytes 98308
  1.0 1.0 %copy-start.2 = (bf16[32,8192]{1,0:T(8,128)(2,1)S(1)}, bf16[32,8192]{1,0:T(8,128)(2,1)}, u32[]{:S(2)}) copy-start(bf16[32,8192]{1,0:T(8,128)(2,1)} %x_ref.1) | copy-start | bytes 1572868
  2.1 0.9 %copy-start.3 = (f32[8,32,32]{2,1,0:T(8,128)S(1)}, f32[8,32,32]{2,1,0:T(8,128)}, u32[]{:S(2)}) copy-start(f32[8,32,32]{2,1,0:T(8,128)} %output_ref.1) | copy-start | bytes 98308
  3.0 0.9 %copy-start.4 = (f32[8,32,32]{2,1,0:T(8,128)S(1)}, f32[8,32,32]{2,1,0:T(8,128)}, u32[]{:S(2)}) copy-start(f32[8,32,32]{2,1,0:T(8,128)} %input_ref.1) | copy-start | bytes 98308
  3.9 0.7 copy-start.6
  15.1 0.8 %copy-start = (bf16[32,8192]{1,0:T(8,128)(2,1)}, bf16[32,8192]{1,0:T(8,128)(2,1)S(1)}, u32[]{:S(2)}) copy-start(bf16[32,8192]{1,0:T(8,128)(2,1)S(1)} %condition.1.x_ref) | copy-start | bytes 1572868
  70.5 1.0 %copy-start.1 = (bf16[16,32,512]{2,1,0:T(8,128)(2,1)S(1)}, bf16[16,32,512]{2,1,0:T(8,128)(2,1)}, u32[]{:S(2)}) copy-start(bf16[16,32,512]{2,1,0:T(8,128)(2,1)} %ring_scores.1.scores_ref) | copy-start | bytes 1572868

commit v4 on v3

--- a/solution.py
+++ b/solution.py
@@ -287,16 +287,16 @@
         base = pl.ds(pl.multiple_of(g * pair, pair), pair)
         width = count // 2
         term = lax.dot_general(
-            held[base, columns], train[n * width : (n + 1) * width, columns],
+            train[n * width : (n + 1) * width, columns], held[base, columns],
             (((1,), (1,)), ((), ())), preferred_element_type=jnp.float32,
         )
         sums = pl.ds(n * width, width)
         if q == 0:
-            total[:, sums] = term
+            total[sums, :] = term
         elif q == 1:
-            total[:, sums] += term
+            total[sums, :] += term
         else:
-            stage[base, sums] = (total[:, sums] + term).astype(jnp.bfloat16)
+            stage[base, sums] = (total[sums, :] + term).T.astype(jnp.bfloat16)
         if q == 2 and n == 1:
             for step in range(2):
                 for d in range(2):
@@ -427,7 +427,7 @@
         scratch_shapes=[
             pltpu.VMEM((blocks * rows, depth), jnp.bfloat16),
             pltpu.VMEM((count, depth), jnp.bfloat16),
-            pltpu.VMEM((4 * rows, count), jnp.float32),
+            pltpu.VMEM((count, 4 * rows), jnp.float32),
             pltpu.VMEM((blocks * rows, count), jnp.bfloat16),
             pltpu.SemaphoreType.DMA,
             pltpu.SemaphoreType.DMA((steps, 2, 4)),

time: 78.3 us -> 78.3 us (level)
  no operation moved by 1% of the time
where the time goes in v4:
time: 78.3 us; the launch traced here: 78 us
  Pallas kernels  71.6 us (91%)
  local copies, waits for them, and re-layouts  6.32 us (8%)
    pallas_call x1, Pallas kernels, ring_scores(): pl.pallas_call(functools.partial(ring_kernel, cores), out_shape=jax.Shape...  54.7 us
    pallas_call x1, Pallas kernels, condition(): pl.pallas_call(functools.partial(condition_kernel, order), grid_spec=pltp...  10.5 us
    pallas_call x1, Pallas kernels, arrange(): pl.pallas_call(arrange_kernel, grid=(blocks // taken,), in_specs=[pl.Bloc...  6.42 us
    unnamed x14, local copies, waits for them, and re-layouts  5.33 us

profile of v4, /device:TPU:0, one launch (start us, length us, event | category | flops | bytes accessed | tf_op | source)
XLA Modules:
  0.0 78.0 jit_solution(333436682013297088)
XLA Ops:
  0.0 0.0 copy-start.5
  0.0 1.0 %reshape.6.eigen_ref = f32[8,8,128]{2,1,0:T(8,128)S(1)} reshape(f32[8,32,32]{2,1,0:T(8,128)} %param.12) | data formatting | bytes 65536 | tf_op jit(solution)/shard_map/reshape | solution.py:115
  1.0 0.0 copy-start.2
  1.0 1.0 %copy-done.2 = bf16[32,8192]{1,0:T(8,128)(2,1)S(1)} copy-done((bf16[32,8192]{1,0:T(8,128)(2,1)S(1)}, bf16[32,8192]{1,0:T(8,128)(2,1)}, u32[]{:S(2)}) %copy-start.2) | copy-done | bytes 524312
  2.1 0.0 copy-start.3
  2.1 0.9 %copy-done.3 = f32[8,32,32]{2,1,0:T(8,128)S(1)} copy-done((f32[8,32,32]{2,1,0:T(8,128)S(1)}, f32[8,32,32]{2,1,0:T(8,128)}, u32[]{:S(2)}) %copy-start.3) | copy-done | bytes 32792
  3.0 0.0 copy-start.4
  3.0 0.9 %copy-done.4 = f32[8,32,32]{2,1,0:T(8,128)S(1)} copy-done((f32[8,32,32]{2,1,0:T(8,128)S(1)}, f32[8,32,32]{2,1,0:T(8,128)}, u32[]{:S(2)}) %copy-start.4) | copy-done | bytes 32792
  3.9 0.0 copy-start.6
  3.9 0.7 copy-done.6
  4.5 10.5 %condition.1.x_ref = bf16[32,8192]{1,0:T(8,128)(2,1)S(1)} custom-call(s32[8]{0:T(128)S(1)} %copy-done.6, bf16[32,8192]{1,0:T(8,128)(2,1)S(1)} %copy-done.2, f32[8,32,32]{2,1,0:T(8,128)S(1)} %copy-done.3, f32[8,32,32]{2,1,0:T(8,128)S(1)} %copy-done.4, f32[8,8,128]{2,1,0:T(8,128)S(1)} %reshape.6.eigen_ref), custom_call_target="tpu_custom_call" | custom-call | tf_op jit(solution)/shard_map/condition/pallas_call | solution.py:99
  15.1 0.0 copy-start
  15.1 0.8 %copy-done = bf16[32,8192]{1,0:T(8,128)(2,1)} copy-done((bf16[32,8192]{1,0:T(8,128)(2,1)}, bf16[32,8192]{1,0:T(8,128)(2,1)S(1)}, u32[]{:S(2)}) %copy-start) | copy-done | bytes 524312
  15.9 54.7 %ring_scores.1.scores_ref = bf16[16,32,512]{2,1,0:T(8,128)(2,1)} custom-call(bf16[32,8192]{1,0:T(8,128)(2,1)} %copy-done, bf16[512,8192]{1,0:T(8,128)(2,1)} %train_hbm.1), custom_call_target="tpu_custom_call" | custom-call | tf_op jit(solution)/shard_map/ring_scores/pallas_call | solution.py:419
  70.5 0.0 copy-done.5
  70.5 0.0 copy-start.1
  70.5 1.0 %copy-done.1 = bf16[16,32,512]{2,1,0:T(8,128)(2,1)S(1)} copy-done((bf16[16,32,512]{2,1,0:T(8,128)(2,1)S(1)}, bf16[16,32,512]{2,1,0:T(8,128)(2,1)}, u32[]{:S(2)}) %copy-start.1) | copy-done | bytes 524312
  71.6 6.4 %arrange.1 = bf16[32,8192]{1,0:T(8,128)(2,1)} custom-call(bf16[16,32,512]{2,1,0:T(8,128)(2,1)S(1)} %copy-done.1, s32[16,1,512]{2,1,0:T(1,128)S(1)} %bitcast.1), custom_call_target="tpu_custom_call" | custom-call | tf_op jit(solution)/shard_map/arrange/pallas_call | solution.py:157
Async XLA Ops:
  0.0 70.5 %copy-start.5 = (s32[8192]{0:T(1024)S(1)}, s32[8192]{0:T(1024)}, u32[]{:S(2)}) copy-start(s32[8192]{0:T(1024)} %param.13) | copy-start | bytes 98308
  1.0 1.0 %copy-start.2 = (bf16[32,8192]{1,0:T(8,128)(2,1)S(1)}, bf16[32,8192]{1,0:T(8,128)(2,1)}, u32[]{:S(2)}) copy-start(bf16[32,8192]{1,0:T(8,128)(2,1)} %x_ref.1) | copy-start | bytes 1572868
  2.1 0.9 %copy-start.3 = (f32[8,32,32]{2,1,0:T(8,128)S(1)}, f32[8,32,32]{2,1,0:T(8,128)}, u32[]{:S(2)}) copy-start(f32[8,32,32]{2,1,0:T(8,128)} %output_ref.1) | copy-start | bytes 98308
  3.0 0.9 %copy-start.4 = (f32[8,32,32]{2,1,0:T(8,128)S(1)}, f32[8,32,32]{2,1,0:T(8,128)}, u32[]{:S(2)}) copy-start(f32[8,32,32]{2,1,0:T(8,128)} %input_ref.1) | copy-start | bytes 98308
  3.9 0.7 copy-start.6
  15.1 0.8 %copy-start = (bf16[32,8192]{1,0:T(8,128)(2,1)}, bf16[32,8192]{1,0:T(8,128)(2,1)S(1)}, u32[]{:S(2)}) copy-start(bf16[32,8192]{1,0:T(8,128)(2,1)S(1)} %condition.1.x_ref) | copy-start | bytes 1572868
  70.5 1.0 %copy-start.1 = (bf16[16,32,512]{2,1,0:T(8,128)(2,1)S(1)}, bf16[16,32,512]{2,1,0:T(8,128)(2,1)}, u32[]{:S(2)}) copy-start(bf16[16,32,512]{2,1,0:T(8,128)(2,1)} %ring_scores.1.scores_ref) | copy-start | bytes 1572868

commit v5 on v3

--- a/solution.py
+++ b/solution.py
@@ -177,7 +177,7 @@
     depth = x_ref.shape[1]
     chips = blocks // cores
     long = chips // 2
-    third = (depth // 3 + WIDE // 2) // WIDE * WIDE
+    third = depth * 3 // 8 // WIDE * WIDE
     slab = lax.axis_index("parts")
     step_rows = 4 * half
     pair = 2 * step_rows

time: 78.3 us -> 78.7 us (level)
  no operation moved by 1% of the time
where the time goes in v5:
time: 78.7 us; the launch traced here: 78.4 us
  Pallas kernels  72 us (91%)
  local copies, waits for them, and re-layouts  6.32 us (8%)
    pallas_call x1, Pallas kernels, ring_scores(): pl.pallas_call(functools.partial(ring_kernel, cores), out_shape=jax.Shape...  55 us
    pallas_call x1, Pallas kernels, condition(): pl.pallas_call(functools.partial(condition_kernel, order), grid_spec=pltp...  10.5 us
    pallas_call x1, Pallas kernels, arrange(): pl.pallas_call(arrange_kernel, grid=(blocks // taken,), in_specs=[pl.Bloc...  6.41 us
    unnamed x14, local copies, waits for them, and re-layouts  5.33 us

profile of v5, /device:TPU:0, one launch (start us, length us, event | category | flops | bytes accessed | tf_op | source)
XLA Modules:
  0.0 78.4 jit_solution(645064530801600968)
XLA Ops:
  0.0 0.0 copy-start.5
  0.0 1.0 %reshape.6.eigen_ref = f32[8,8,128]{2,1,0:T(8,128)S(1)} reshape(f32[8,32,32]{2,1,0:T(8,128)} %param.12) | data formatting | bytes 65536 | tf_op jit(solution)/shard_map/reshape | solution.py:115
  1.0 0.0 copy-start.2
  1.0 1.0 %copy-done.2 = bf16[32,8192]{1,0:T(8,128)(2,1)S(1)} copy-done((bf16[32,8192]{1,0:T(8,128)(2,1)S(1)}, bf16[32,8192]{1,0:T(8,128)(2,1)}, u32[]{:S(2)}) %copy-start.2) | copy-done | bytes 524312
  2.1 0.0 copy-start.3
  2.1 0.9 %copy-done.3 = f32[8,32,32]{2,1,0:T(8,128)S(1)} copy-done((f32[8,32,32]{2,1,0:T(8,128)S(1)}, f32[8,32,32]{2,1,0:T(8,128)}, u32[]{:S(2)}) %copy-start.3) | copy-done | bytes 32792
  3.0 0.0 copy-start.4
  3.0 0.9 %copy-done.4 = f32[8,32,32]{2,1,0:T(8,128)S(1)} copy-done((f32[8,32,32]{2,1,0:T(8,128)S(1)}, f32[8,32,32]{2,1,0:T(8,128)}, u32[]{:S(2)}) %copy-start.4) | copy-done | bytes 32792
  3.9 0.0 copy-start.6
  3.9 0.7 copy-done.6
  4.5 10.5 %condition.1.x_ref = bf16[32,8192]{1,0:T(8,128)(2,1)S(1)} custom-call(s32[8]{0:T(128)S(1)} %copy-done.6, bf16[32,8192]{1,0:T(8,128)(2,1)S(1)} %copy-done.2, f32[8,32,32]{2,1,0:T(8,128)S(1)} %copy-done.3, f32[8,32,32]{2,1,0:T(8,128)S(1)} %copy-done.4, f32[8,8,128]{2,1,0:T(8,128)S(1)} %reshape.6.eigen_ref), custom_call_target="tpu_custom_call" | custom-call | tf_op jit(solution)/shard_map/condition/pallas_call | solution.py:99
  15.1 0.0 copy-start
  15.1 0.8 %copy-done = bf16[32,8192]{1,0:T(8,128)(2,1)} copy-done((bf16[32,8192]{1,0:T(8,128)(2,1)}, bf16[32,8192]{1,0:T(8,128)(2,1)S(1)}, u32[]{:S(2)}) %copy-start) | copy-done | bytes 524312
  15.9 55.0 %ring_scores.1.scores_ref = bf16[16,32,512]{2,1,0:T(8,128)(2,1)} custom-call(bf16[32,8192]{1,0:T(8,128)(2,1)} %copy-done, bf16[512,8192]{1,0:T(8,128)(2,1)} %train_hbm.1), custom_call_target="tpu_custom_call" | custom-call | tf_op jit(solution)/shard_map/ring_scores/pallas_call | solution.py:419
  70.9 0.0 copy-done.5
  70.9 0.0 copy-start.1
  70.9 1.0 %copy-done.1 = bf16[16,32,512]{2,1,0:T(8,128)(2,1)S(1)} copy-done((bf16[16,32,512]{2,1,0:T(8,128)(2,1)S(1)}, bf16[16,32,512]{2,1,0:T(8,128)(2,1)}, u32[]{:S(2)}) %copy-start.1) | copy-done | bytes 524312
  71.9 6.4 %arrange.1 = bf16[32,8192]{1,0:T(8,128)(2,1)} custom-call(bf16[16,32,512]{2,1,0:T(8,128)(2,1)S(1)} %copy-done.1, s32[16,1,512]{2,1,0:T(1,128)S(1)} %bitcast.1), custom_call_target="tpu_custom_call" | custom-call | tf_op jit(solution)/shard_map/arrange/pallas_call | solution.py:157
Async XLA Ops:
  0.0 70.9 %copy-start.5 = (s32[8192]{0:T(1024)S(1)}, s32[8192]{0:T(1024)}, u32[]{:S(2)}) copy-start(s32[8192]{0:T(1024)} %param.13) | copy-start | bytes 98308
  1.0 1.0 %copy-start.2 = (bf16[32,8192]{1,0:T(8,128)(2,1)S(1)}, bf16[32,8192]{1,0:T(8,128)(2,1)}, u32[]{:S(2)}) copy-start(bf16[32,8192]{1,0:T(8,128)(2,1)} %x_ref.1) | copy-start | bytes 1572868
  2.1 0.9 %copy-start.3 = (f32[8,32,32]{2,1,0:T(8,128)S(1)}, f32[8,32,32]{2,1,0:T(8,128)}, u32[]{:S(2)}) copy-start(f32[8,32,32]{2,1,0:T(8,128)} %output_ref.1) | copy-start | bytes 98308
  3.0 0.9 %copy-start.4 = (f32[8,32,32]{2,1,0:T(8,128)S(1)}, f32[8,32,32]{2,1,0:T(8,128)}, u32[]{:S(2)}) copy-start(f32[8,32,32]{2,1,0:T(8,128)} %input_ref.1) | copy-start | bytes 98308
  3.9 0.7 copy-start.6
  15.1 0.8 %copy-start = (bf16[32,8192]{1,0:T(8,128)(2,1)}, bf16[32,8192]{1,0:T(8,128)(2,1)S(1)}, u32[]{:S(2)}) copy-start(bf16[32,8192]{1,0:T(8,128)(2,1)S(1)} %condition.1.x_ref) | copy-start | bytes 1572868
  70.9 1.0 %copy-start.1 = (bf16[16,32,512]{2,1,0:T(8,128)(2,1)S(1)}, bf16[16,32,512]{2,1,0:T(8,128)(2,1)}, u32[]{:S(2)}) copy-start(bf16[16,32,512]{2,1,0:T(8,128)(2,1)} %ring_scores.1.scores_ref) | copy-start | bytes 1572868
